TPU v7x, 32 devices: a whole 2x2x4 slice. The times are simulated.
32 devices in a mesh: ia: 4 (over y, x), ja: 8 (over z, core), ka: 1.
Axes of the slice: x: 2, y: 2, z: 4, core: 2. Of those that a mesh axis runs over, the one named last changes fastest.
Arguments:
- tensor: bfloat16 [8, 2048, 4096], P('ka', 'ia', 'ja'), may hold values from -6 to 6
- factor_b: float32 [32, 4096], P('ia', ('ja', 'ka')), may hold values from -0.09375 to 0.09375
- factor_c: float32 [32, 8], P(('ia', 'ja'), 'ka'), may hold values from -2 to 2
Outputs:
- factor_a_new: float32 [32, 2048], P('ja', ('ia', 'ka'))
- factor_b_new: float32 [32, 4096], P('ia', ('ja', 'ka'))
All inputs are finite; a program needn't handle non-finite values.
Results may differ from a plain program's by a relative error of at most 0.0033.
Values sent between devices are 32-bit elements; how exact they have to be, the bound alone decides.
A program may use at most 64 MiB of HBM per device.

v0:
```python
import jax
import jax.numpy as jnp
from jax import lax
from jax.sharding import PartitionSpec as P

EPS = 1e-06
HIGH = lax.Precision.HIGHEST


def gram_of(block):
    return jnp.dot(block, block.T, precision=HIGH, preferred_element_type=jnp.float32)


def solve_with(normal, rhs):
    lower = jnp.linalg.cholesky(normal)
    return jax.scipy.linalg.cho_solve((lower, True), rhs)


def arrange(partial_rows, rows_split, cols_split):
    rank, width = partial_rows.shape
    grid = partial_rows.reshape(rows_split, rank // rows_split, cols_split, width // cols_split)
    return grid.transpose(0, 2, 1, 3).reshape(rank * cols_split, width // cols_split)


def assemble(pieces, rows_split, cols_split):
    count, height, width = pieces.shape
    grid = pieces.reshape(rows_split, cols_split, height, width)
    return grid.transpose(0, 2, 1, 3).reshape(rows_split * height, cols_split * width)


def scaled(raw, squares, total):
    return raw / jnp.sqrt(squares / total + EPS)[:, None]


def body(tensor, factor_b, factor_c):
    n_ia = lax.axis_size("ia")
    n_ja = lax.axis_size("ja")
    n_ka = lax.axis_size("ka")
    total_i = tensor.shape[1] * n_ia
    total_j = tensor.shape[2] * n_ja
    c_block = lax.all_gather(factor_c, ("ia", "ja"), axis=0, tiled=True)
    pieces = lax.all_gather(factor_b[None], ("ia", "ka"), axis=0, tiled=True)
    b_block = assemble(pieces, n_ia, n_ka)
    gram_b = lax.psum(gram_of(b_block), "ja")
    gram_c = lax.psum(gram_of(c_block), "ka")
    normal_a = gram_b * gram_c
    kr_a = (c_block[:, :, None] * b_block[:, None, :]).astype(jnp.bfloat16)
    partial_a = jnp.einsum("rkj,kij->ri", kr_a, tensor, preferred_element_type=jnp.float32)
    solved_a = solve_with(normal_a, partial_a)
    raw_a = lax.psum_scatter(
        arrange(solved_a, n_ja, n_ka), ("ja", "ka"), scatter_dimension=0, tiled=True
    )
    squares_a = lax.psum(jnp.sum(raw_a * raw_a, axis=1), ("ia", "ka"))
    local_a = scaled(raw_a, squares_a, total_i)
    pieces_a = lax.all_gather(local_a[None], ("ja", "ka"), axis=0, tiled=True)
    gathered_a = assemble(pieces_a, n_ja, n_ka)
    gram_a = lax.psum(gram_of(gathered_a), "ia")
    normal_b = gram_a * gram_c
    kr_b = (c_block[:, :, None] * gathered_a[:, None, :]).astype(jnp.bfloat16)
    partial_b = jnp.einsum("rki,kij->rj", kr_b, tensor, preferred_element_type=jnp.float32)
    solved_b = solve_with(normal_b, partial_b)
    raw_b = lax.psum_scatter(
        arrange(solved_b, n_ia, n_ka), ("ia", "ka"), scatter_dimension=0, tiled=True
    )
    squares_b = lax.psum(jnp.sum(raw_b * raw_b, axis=1), ("ja", "ka"))
    share_b = scaled(raw_b, squares_b, total_j)
    return (local_a, share_b)


def solution(mesh):
    return jax.shard_map(
        body,
        mesh=mesh,
        in_specs=(P("ka", "ia", "ja"), P("ia", ("ja", "ka")), P(("ia", "ja"), "ka")),
        out_specs=(P("ja", ("ia", "ka")), P("ia", ("ja", "ka"))),
        check_vma=False,
    )
```

profile of v0, /device:TPU:0, one launch (start us, length us, event | category | flops | bytes accessed | tf_op | source)
XLA Modules:
  0.0 263.4 jit_solution(10724994050530571382)
XLA Ops:
  7.2 0.0 copy-start.1
  7.2 0.0 all-reduce.5.cloned.1.call-start
  7.2 43.2 %all-gather.2 = f32[32,1,8]{2,1,0:T(1,128)S(1)} all-gather(f32[1,1,8]{2,1,0:T(1,128)} %bitcast.47), channel_id=1, replica_groups=mesh['ia'=4,'ja'=8,'ka'=1] {'ia','ja'}, dimensions={0}, use_global_device_ids=true | all-gather | bytes 1056 | tf_op jit(solution)/shard_map/all_gather | solution.py:41
  50.4 7.4 %all-gather = f32[32,512]{1,0:T(8,128)S(1)} all-gather(f32[8,512]{1,0:T(8,128)} %param.7), channel_id=2, replica_groups=mesh['ia'=4,'ja'=8,'ka'=1] {'ia','ka'}, dimensions={0}, use_global_device_ids=true | all-gather | bytes 81920 | tf_op jit(solution)/shard_map/all_gather | solution.py:42
  57.9 0.2 fusion.15
  58.1 25.9 %psum.31 = f32[32,32]{0,1:T(8,128)S(1)} all-reduce(f32[32,32]{0,1:T(8,128)S(1)} %fusion.15), channel_id=1, replica_groups=mesh['ia'=4,'ja'=8,'ka'=1] {'ja'}, use_global_device_ids=true, to_apply=%region_0.0 | all-reduce | flops 1024 | bytes 8192 | tf_op jit(solution)/shard_map/psum | solution.py:44
  84.0 0.1 multiply_convert_fusion.1
  84.1 0.1 fusion.14
  84.2 0.1 copy.13
  84.3 2.9 %cholesky.44 = f32[32,32]{1,0:T(8,128)S(1)} custom-call(f32[32,32]{1,0:T(8,128)S(1)} %fusion.13), custom_call_target="Cholesky" | custom-call | tf_op jit(solution)/shard_map/jit(cholesky)/cholesky | solution.py:15
  87.3 0.6 compare_reduce_fusion.1
  87.9 0.7 fusion.2
  88.6 2.4 custom-call.8
  91.0 3.5 %convolution_bitcast_fusion.1 = f32[32,512]{1,0:T(8,128)S(1)} fusion(bf16[8,512,512]{2,1,0:T(8,128)(2,1)} %param.6, bf16[32,8,512]{2,1,0:T(8,128)(2,1)S(1)} %multiply_convert_fusion.1), kind=kOutput, calls=%fused_computation.1 | convolution fusion | flops 134217728 | bytes 4521984 | tf_op jit(solution)/shard_map/rkj,kij->ri/dot_general | solution.py:48
  94.5 0.0 copy-start
  94.5 0.3 fusion.11
  94.8 0.8 fusion.9
  95.6 0.0 all-reduce.5.cloned.1.call-update
  95.6 0.0 all-reduce.7.cloned.1.call-start
  95.7 0.0 copy-done.1
  95.7 0.6 dynamic-slice
  96.9 49.7 %all-reduce.5.cloned.1.call-done = f32[32,512]{1,0:T(8,128)} async-done(((f32[32,512]{1,0:T(8,128)}), f32[32,512]{1,0:T(8,128)}) %all-reduce.5.cloned.1.call-update) | async-done | bytes 65552
  146.7 0.8 multiply_reduce_fusion.1
  147.5 9.8 %psum.32 = f32[4]{0:T(128)S(1)} all-reduce(f32[4]{0:T(128)S(1)} %multiply_reduce_fusion.1), channel_id=1, replica_groups=mesh['ia'=4,'ja'=8,'ka'=1] {'ia','ka'}, use_global_device_ids=true, to_apply=%region_5.0 | all-reduce | flops 4 | bytes 32 | tf_op jit(solution)/shard_map/psum | solution.py:53
  157.3 0.8 fusion.29
  158.1 14.0 %all-gather.3 = f32[8,4,512]{2,1,0:T(4,128)S(1)} all-gather(f32[1,4,512]{2,1,0:T(4,128)S(1)} %fusion.29), channel_id=3, replica_groups=mesh['ia'=4,'ja'=8,'ka'=1] {'ja','ka'}, dimensions={0}, use_global_device_ids=true | all-gather | bytes 73728 | tf_op jit(solution)/shard_map/all_gather | solution.py:55
  172.1 0.2 fusion.16
  172.3 0.1 multiply_convert_fusion
  172.4 14.1 %psum.33 = f32[32,32]{0,1:T(8,128)S(1)} all-reduce(f32[32,32]{0,1:T(8,128)S(1)} %fusion.16), channel_id=1, replica_groups=mesh['ia'=4,'ja'=8,'ka'=1] {'ia'}, use_global_device_ids=true, to_apply=%region_6.0 | all-reduce | flops 1024 | bytes 8192 | tf_op jit(solution)/shard_map/psum | solution.py:57
  186.6 0.1 copy.16
  186.6 2.9 %cholesky.55 = f32[32,32]{1,0:T(8,128)S(1)} custom-call(f32[32,32]{1,0:T(8,128)S(1)} %fusion.8), custom_call_target="Cholesky" | custom-call | tf_op jit(solution)/shard_map/jit(cholesky)/cholesky | solution.py:15
  189.6 0.6 compare_reduce_fusion
  190.2 0.7 fusion.3
  190.9 2.5 custom-call.9
  193.4 2.9 %convolution_bitcast_fusion = f32[32,512]{1,0:T(8,128)S(1)} fusion(bf16[8,512,512]{2,1,0:T(8,128)(2,1)} %param.6, bf16[32,8,512]{2,1,0:T(8,128)(2,1)S(1)} %multiply_convert_fusion), kind=kOutput, calls=%fused_computation | convolution fusion | flops 134217728 | bytes 4521984 | tf_op jit(solution)/shard_map/rki,kij->rj/dot_general | solution.py:60
  196.2 0.3 fusion.6
  196.5 0.8 fusion.4
  197.3 0.0 all-reduce.7.cloned.1.call-update
  197.3 0.0 copy-done
  197.3 0.6 dynamic-slice.2
  198.6 38.4 %all-reduce.7.cloned.1.call-done = f32[32,512]{1,0:T(8,128)} async-done(((f32[32,512]{1,0:T(8,128)}), f32[32,512]{1,0:T(8,128)}) %all-reduce.7.cloned.1.call-update) | async-done | bytes 65552
  237.0 0.8 multiply_reduce_fusion
  237.8 1.4 dynamic-slice_divide_fusion.1
  239.2 16.0 %psum.34 = f32[8]{0:T(128)S(1)} all-reduce(f32[8]{0:T(128)S(1)} %multiply_reduce_fusion), channel_id=1, replica_groups=mesh['ia'=4,'ja'=8,'ka'=1] {'ja','ka'}, use_global_device_ids=true, to_apply=%region_9.12 | all-reduce | flops 8 | bytes 64 | tf_op jit(solution)/shard_map/psum | solution.py:65
  255.2 1.4 dynamic-slice_divide_fusion
  (8 shorter events, 0.1 us)
Async XLA Ops:
  7.2 88.5 %copy-start.1 = (u32[32]{0:T(128)S(1)}, u32[32]{0:T(128)}, u32[]{:S(2)}) copy-start(u32[32]{0:T(128)} %constant.49) | copy-start | bytes 388
  7.2 139.5 %all-reduce.5.cloned.1.call-start = ((), (), s32[]{:S(2)}) async-start(), calls=%async_computation | async-start | bytes 131072
  94.5 102.8 %copy-start = (u32[32]{0:T(128)S(1)}, u32[32]{0:T(128)}, u32[]{:S(2)}) copy-start(u32[32]{0:T(128)} %constant.53) | copy-start | bytes 388
  95.6 141.3 %all-reduce.7.cloned.1.call-start = ((), (), s32[]{:S(2)}) async-start(), calls=%async_computation.1 | async-start | bytes 131072
Sparse Core Ops, SparseCore 0:
  95.8 50.8 all-reduce.4
  197.4 39.4 all-reduce.6
where the time goes:
time: 264 us; the launch traced here: 263 us
  blocking collectives  130 us (49%)
  waiting for transfers between devices  88.1 us (33%)
  other arithmetic  18.9 us (7%)
  between operations  15.5 us (6%)
  matrix products  9.08 us (3%)
    unnamed x4, waiting for transfers between devices  88.1 us
    all_gather x1, blocking collectives, body(): c_block = lax.all_gather(factor_c, ('ia', 'ja'), axis=0, tiled=True)  43.2 us
    psum x1, blocking collectives, body(): gram_b = lax.psum(gram_of(b_block), 'ja')  25.9 us
    psum x1, blocking collectives, body(): squares_b = lax.psum(jnp.sum(raw_b * raw_b, axis=1), ('ja', 'ka'))  16 us
    psum x1, blocking collectives, body(): gram_a = lax.psum(gram_of(gathered_a), 'ia')  14.1 us
    all_gather x1, blocking collectives, body(): pieces_a = lax.all_gather(local_a[None], ('ja', 'ka'), axis=0, tiled=True)  14 us
    psum x1, blocking collectives, body(): squares_a = lax.psum(jnp.sum(raw_a * raw_a, axis=1), ('ia', 'ka'))  9.84 us
    all_gather x1, blocking collectives, body(): pieces = lax.all_gather(factor_b[None], ('ia', 'ka'), axis=0, tiled=True)  7.41 us
  transfers between devices with their start and end apart: 2, of which 2 were waited for; matrix products, arithmetic and copies ran while one was open for 0% of the time, Pallas kernels for 0%

commit v1 on v0

--- a/solution.py
+++ b/solution.py
@@ -1,6 +1,10 @@
+import functools
+
 import jax
 import jax.numpy as jnp
 from jax import lax
+from jax.experimental import pallas as pl
+from jax.experimental.pallas import tpu as pltpu
 from jax.sharding import PartitionSpec as P
 
 EPS = 1e-06
@@ -67,9 +71,312 @@
     return (local_a, share_b)
 
 
+MESH = pl.DeviceIdType.MESH
+LANES = 128
+SUBS = 8
+NT = (((1,), (1,)), ((), ()))
+
+
+def spread(src, dst, me, count, device, send, recv):
+    copies = []
+    for step in range(1, count):
+        copies.append(
+            pltpu.make_async_remote_copy(
+                src_ref=src,
+                dst_ref=dst.at[me],
+                send_sem=send.at[step],
+                recv_sem=recv.at[step],
+                device_id=device(lax.rem(me + step, count)),
+                device_id_type=MESH,
+            )
+        )
+    return copies
+
+
+def stacked(pieces, rows):
+    height, width = sum(p.shape[0] for p in pieces), pieces[0].shape[1]
+    if rows > height:
+        pieces = list(pieces) + [jnp.zeros((rows - height, width), pieces[0].dtype)]
+    return jnp.concatenate(pieces, axis=0)
+
+
+def wide_gram(block):
+    other = stacked([block], LANES)
+    return lax.dot_general(block, other, NT, precision=HIGH, preferred_element_type=jnp.float32)
+
+
+def packed(gram):
+    rank = gram.shape[0]
+    tile = gram[0:SUBS]
+    for q in range(1, rank // SUBS):
+        tile = tile + pltpu.roll(gram[q * SUBS : (q + 1) * SUBS], q * rank, 1)
+    return tile
+
+
+def unpacked(tile, rank):
+    lane = lax.broadcasted_iota(jnp.int32, (SUBS, LANES), 1)
+    groups = []
+    for q in range(rank // SUBS):
+        moved = tile if q == 0 else pltpu.roll(tile, LANES - q * rank, 1)
+        groups.append(jnp.where(lane < rank, moved, 0.0))
+    return jnp.concatenate(groups, axis=0)
+
+
+def inverse(normal):
+    rank = normal.shape[0]
+    lane = lax.broadcasted_iota(jnp.int32, normal.shape, 1)
+    sub = lax.broadcasted_iota(jnp.int32, normal.shape, 0)
+    for k in range(rank):
+        col = normal[:, k : k + 1]
+        row = normal[k : k + 1, :]
+        pivot = 1.0 / normal[k : k + 1, k : k + 1]
+        row = jnp.where(lane[0:1] == k, 1.0, row) * pivot
+        rest = jnp.where(lane == k, 0.0, normal) - col * row
+        normal = jnp.where(sub == k, row, rest)
+    return normal
+
+
+def split(values):
+    high = values.astype(jnp.bfloat16).astype(jnp.float32)
+    return high, values - high
+
+
+def kernel(
+    n_ia, n_ja, total_i, total_j,
+    t_ref, b_ref, c_ref, oa_ref, ob_ref,
+    tv, ball, cst, cja, cia, gb, pbuf, ra, ga, araw, gr, rb, wsc, sq,
+    t_sem, b_s, b_r, cj_s, cj_r, ci_s, ci_r, gb_s, gb_r, ra_s, ra_r, ga_s, ga_r,
+    gr_s, gr_r, rb_s, rb_r, sq_s, sq_r,
+):
+    a = lax.axis_index("ia")
+    j = lax.axis_index("ja")
+    steps, width_i, width_j = tv.shape
+    rank = n_ia * b_ref.shape[0]
+    groups = rank // SUBS
+    halves = n_ja // groups
+    part_i = width_i // halves
+    cuts_j = rb.shape[0]
+    part_j = width_j // cuts_j
+
+    def on_ia(index):
+        return (index, j, 0)
+
+    def on_ja(index):
+        return (a, index, 0)
+
+    loads = []
+    for h in range(halves):
+        rows = pl.ds(h * part_i, part_i)
+        load = pltpu.make_async_copy(t_ref.at[:, rows], tv.at[:, rows], t_sem.at[h])
+        load.start()
+        loads.append(load)
+
+    barrier = pltpu.get_barrier_semaphore()
+    for step in range(1, n_ia):
+        pl.semaphore_signal(barrier, inc=1, device_id=on_ia(lax.rem(a + step, n_ia)), device_id_type=MESH)
+    for step in range(1, n_ja):
+        pl.semaphore_signal(barrier, inc=1, device_id=on_ja(lax.rem(j + step, n_ja)), device_id_type=MESH)
+    cst[...] = jnp.zeros_like(cst)
+    cst[0:1, 0:steps] = c_ref[...]
+    cja[j] = cst[...]
+    ball[a] = b_ref[...]
+    pl.semaphore_wait(barrier, n_ia + n_ja - 2)
+
+    sends = []
+
+    def begin(copies):
+        for copy in copies:
+            copy.start()
+        sends.extend(copies)
+        return copies
+
+    def arrived(copies):
+        for copy in copies:
+            copy.wait_recv()
+
+    b_copies = begin(spread(b_ref, ball, a, n_ia, on_ia, b_s, b_r))
+    cj_copies = begin(spread(cst, cja, j, n_ja, on_ja, cj_s, cj_r))
+    arrived(cj_copies)
+    cia[a] = stacked([cja[s, 0:1, :] for s in range(n_ja)], n_ja)
+    ci_copies = begin(spread(cia.at[a], cia, a, n_ia, on_ia, ci_s, ci_r))
+    arrived(b_copies)
+    b_all = stacked([ball[s] for s in range(n_ia)], rank)
+    gb[j] = packed(wide_gram(b_all))
+    gb_copies = begin(spread(gb.at[j], gb, j, n_ja, on_ja, gb_s, gb_r))
+    weights = stacked(list(split(b_all)), LANES).T.astype(jnp.bfloat16)
+    arrived(ci_copies)
+    c_all = stacked([cia[s] for s in range(n_ia)], rank)
+    gram_c = wide_gram(c_all)
+    c_rows = stacked([c_all, c_all], LANES).T
+
+    ra_copies = []
+    for step in range(1, n_ja):
+        peer = lax.rem(j + step, n_ja)
+        ra_copies.append(
+            pltpu.make_async_remote_copy(
+                src_ref=pbuf.at[peer],
+                dst_ref=ra.at[j],
+                send_sem=ra_s.at[step],
+                recv_sem=ra_r.at[step],
+                device_id=on_ja(peer),
+                device_id_type=MESH,
+            )
+        )
+    for h in range(halves):
+        loads[h].wait()
+        total = jnp.zeros((part_i, LANES), jnp.float32)
+        for k in range(steps):
+            product = jnp.dot(
+                tv[k, h * part_i : (h + 1) * part_i, :], weights, preferred_element_type=jnp.float32
+            )
+            total = total + product * c_rows[k : k + 1, :]
+        total = total.T
+        total = total[0:rank] + total[rank : 2 * rank]
+        for q in range(groups):
+            pbuf[q * halves + h] = total[q * SUBS : (q + 1) * SUBS]
+        for step in range(1, n_ja):
+            @pl.when(lax.rem(j + step, halves) == h)
+            def _():
+                ra_copies[step - 1].start()
+    sends.extend(ra_copies)
+    ra[j] = pbuf[j]
+
+    arrived(gb_copies)
+    gram_b = unpacked(functools.reduce(jnp.add, [gb[s] for s in range(n_ja)]), rank)
+    solve_a = inverse(gram_b * gram_c)
+
+    arrived(ra_copies)
+    ga[j] = functools.reduce(jnp.add, [ra[s] for s in range(n_ja)])
+    ga_copies = begin(spread(ga.at[j], ga, j, n_ja, on_ja, ga_s, ga_r))
+    c_cols = [c_all[:, k : k + 1] for k in range(steps)]
+    arrived(ga_copies)
+    summed = stacked(
+        [
+            jnp.concatenate([ga[q * halves + h] for h in range(halves)], axis=1)
+            for q in range(groups)
+        ],
+        rank,
+    )
+    raw_a = jnp.dot(solve_a[:, 0:rank], summed, precision=HIGH, preferred_element_type=jnp.float32)
+    araw[...] = raw_a
+    gr[a] = packed(wide_gram(raw_a))
+    gr_copies = begin(spread(gr.at[a], gr, a, n_ia, on_ia, gr_s, gr_r))
+
+    rb_copies = []
+    pieces = []
+    for k in range(steps):
+        pieces.append(jnp.concatenate(split(raw_a * c_cols[k]), axis=0).astype(jnp.bfloat16))
+    for h in range(cuts_j):
+        total = jnp.zeros((2 * rank, part_j), jnp.float32)
+        for k in range(steps):
+            total = total + jnp.dot(
+                pieces[k], tv[k, :, h * part_j : (h + 1) * part_j], preferred_element_type=jnp.float32
+            )
+        rb[h, a] = total[0:rank] + total[rank : 2 * rank]
+        rb_copies.extend(
+            begin(spread(rb.at[h, a], rb.at[h], a, n_ia, on_ia, rb_s.at[h], rb_r.at[h]))
+        )
+
+    arrived(gr_copies)
+    gram_a = unpacked(functools.reduce(jnp.add, [gr[s] for s in range(n_ia)]), rank)
+    lane = lax.broadcasted_iota(jnp.int32, (rank, LANES), 1)
+    sub = lax.broadcasted_iota(jnp.int32, (rank, LANES), 0)
+    squares = jnp.where(lane == sub, gram_a, 0.0)
+    scale_col = 1.0 / jnp.sqrt(jnp.sum(squares, axis=1, keepdims=True) / total_i + EPS)
+    scale_row = 1.0 / jnp.sqrt(jnp.sum(squares, axis=0, keepdims=True) / total_i + EPS)
+    solve_b = inverse(gram_a * scale_col * scale_row * gram_c) * scale_row
+    for q in range(n_ia):
+        wsc[q] = solve_b[q * SUBS : (q + 1) * SUBS]
+    new_a = araw[...] * scale_col
+    for q in range(groups):
+        araw[q * SUBS : (q + 1) * SUBS] = new_a[q * SUBS : (q + 1) * SUBS]
+    height = rank // n_ja
+    for p in range(n_ja):
+        @pl.when(j == p)
+        def _():
+            oa_ref[...] = araw[p * height : (p + 1) * height, :]
+    solve_own = wsc[a][:, 0:rank]
+
+    arrived(rb_copies)
+    raw_b = []
+    for h in range(cuts_j):
+        summed_b = functools.reduce(jnp.add, [rb[h, s] for s in range(n_ia)])
+        raw_b.append(
+            jnp.dot(solve_own, summed_b, precision=HIGH, preferred_element_type=jnp.float32)
+        )
+    raw_b = jnp.concatenate(raw_b, axis=1)
+    sq[j] = jnp.broadcast_to(jnp.sum(raw_b * raw_b, axis=1, keepdims=True), (SUBS, LANES))
+    sq_copies = begin(spread(sq.at[j], sq, j, n_ja, on_ja, sq_s, sq_r))
+    arrived(sq_copies)
+    squares_b = functools.reduce(jnp.add, [sq[s] for s in range(n_ja)])[:, 0:1]
+    ob_ref[...] = raw_b / jnp.sqrt(squares_b / total_j + EPS)
+
+    for copy in sends:
+        copy.wait_send()
+
+
+def fused(tensor, factor_b, factor_c):
+    n_ia = lax.axis_size("ia")
+    n_ja = lax.axis_size("ja")
+    steps, width_i, width_j = tensor.shape
+    rows_b = factor_b.shape[0]
+    rank = rows_b * n_ia
+    halves = n_ja // (rank // SUBS)
+    cuts_j = 2
+    f32 = jnp.float32
+    vmem = pltpu.VMEM
+    dma = pltpu.SemaphoreType.DMA
+    ja_sems = [dma((n_ja,)), dma((n_ja,))]
+    ia_sems = [dma((n_ia,)), dma((n_ia,))]
+    scratch = [
+        vmem(tensor.shape, tensor.dtype),
+        vmem((n_ia, rows_b, width_j), f32),
+        vmem((SUBS, LANES), f32),
+        vmem((n_ja, SUBS, LANES), f32),
+        vmem((n_ia, n_ja, LANES), f32),
+        vmem((n_ja, SUBS, LANES), f32),
+        vmem((n_ja, SUBS, width_i // halves), f32),
+        vmem((n_ja, SUBS, width_i // halves), f32),
+        vmem((n_ja, SUBS, width_i // halves), f32),
+        vmem((rank, width_i), f32),
+        vmem((n_ia, SUBS, LANES), f32),
+        vmem((cuts_j, n_ia, rank, width_j // cuts_j), f32),
+        vmem((n_ia, SUBS, LANES), f32),
+        vmem((n_ja, SUBS, LANES), f32),
+        dma((halves,)),
+        *ia_sems, *ja_sems, *ia_sems, *ja_sems, *ja_sems, *ja_sems, *ia_sems,
+        dma((cuts_j, n_ia)), dma((cuts_j, n_ia)),
+        *ja_sems,
+    ]
+    flops = 8 * rank * tensor.size
+    return pl.pallas_call(
+        functools.partial(kernel, n_ia, n_ja, width_i * n_ia, width_j * n_ja),
+        out_shape=(
+            jax.ShapeDtypeStruct((rank // n_ja, width_i), f32),
+            jax.ShapeDtypeStruct((rows_b, width_j), f32),
+        ),
+        in_specs=[
+            pl.BlockSpec(memory_space=pl.ANY),
+            pl.BlockSpec(memory_space=pltpu.VMEM),
+            pl.BlockSpec(memory_space=pltpu.VMEM),
+        ],
+        out_specs=(pl.BlockSpec(memory_space=pltpu.VMEM), pl.BlockSpec(memory_space=pltpu.VMEM)),
+        scratch_shapes=scratch,
+        cost_estimate=pl.CostEstimate(flops=flops, bytes_accessed=2 * tensor.size, transcendentals=0),
+        compiler_params=pltpu.CompilerParams(
+            collective_id=0, has_side_effects=True, vmem_limit_bytes=40 * 2**20
+        ),
+    )(tensor, factor_b, factor_c)
+
+
+def fits(mesh):
+    n_ia, n_ja, n_ka = (mesh.shape[name] for name in ("ia", "ja", "ka"))
+    return n_ka == 1 and n_ia * SUBS == 32 and n_ja % n_ia == 0 and n_ja <= SUBS
+
+
 def solution(mesh):
     return jax.shard_map(
-        body,
+        fused if fits(mesh) else body,
         mesh=mesh,
         in_specs=(P("ka", "ia", "ja"), P("ia", ("ja", "ka")), P(("ia", "ja"), "ka")),
         out_specs=(P("ja", ("ia", "ka")), P("ia", ("ja", "ka"))),

time: 264 us -> 38.1 us (0.14)
  blocking collectives: 130 us -> 0 us
  waiting for transfers between devices: 88.1 us -> 0 us
  Pallas kernels: 0 us -> 32.5 us
  other arithmetic: 18.9 us -> 0 us
  between operations: 15.5 us -> 0.65 us
  matrix products: 9.08 us -> 0 us
  local copies, waits for them, and re-layouts: 1.35 us -> 4.76 us
    unnamed x4 -> x0, waiting for transfers between devices: 88.1 us -> none
    psum x4 -> x0, blocking collectives: 65.8 us -> none  [the longest x1 25.9 us: body(): gram_b = lax.psum(gram_of(b_block), 'ja')]
    all_gather x3 -> x0, blocking collectives: 64.6 us -> none  [the longest x1 43.2 us: body(): c_block = lax.all_gather(factor_c, ('ia', 'ja'), axis=0, tiled=True)]
    pallas_call x0 -> x1, Pallas kernels: none -> 32.5 us  [fused(): pl.pallas_call(functools.partial(kernel, n_ia, n_ja, width_i * n_ia, widt...]
    another operation x10 -> x0, other arithmetic: 13.4 us -> none  [the longest x6 7.19 us: solve_with(): lower = jnp.linalg.cholesky(normal)]
    dot_general x5 -> x0, matrix products: 6.91 us -> none  [the longest x1 3.52 us: body(): jnp.einsum('rkj,kij->ri', kr_a, tensor, preferred_element_type=jnp.float32)]
    unnamed x7 -> x8, local copies, waits for them, and re-layouts: 1.21 us -> 4.76 us
    div x4 -> x0, other arithmetic: 2.81 us -> none  [the longest x2 2.79 us: scaled(): return raw / jnp.sqrt(squares / total + EPS)[:, None]]
  transfers between devices with their start and end apart: 2 -> 0, of which waited for: 2 -> 0; matrix products, arithmetic and copies ran while one was open for 0% -> 0% of each run, Pallas kernels for 0% -> 0%
where the time goes in v1:
time: 38.1 us; the launch traced here: 37.9 us
  Pallas kernels  32.5 us (85%)
  local copies, waits for them, and re-layouts  4.76 us (12%)
  between operations  0.65 us (2%)
    pallas_call x1, Pallas kernels, fused(): pl.pallas_call(functools.partial(kernel, n_ia, n_ja, width_i * n_ia, widt...  32.5 us
    unnamed x8, local copies, waits for them, and re-layouts  4.76 us

profile of v1, /device:TPU:0, one launch (start us, length us, event | category | flops | bytes accessed | tf_op | source)
XLA Modules:
  0.0 37.9 jit_solution(2508966563148524432)
XLA Ops:
  0.6 0.0 copy-start
  0.6 2.2 %copy-done = bf16[8,512,512]{2,1,0:T(8,128)(2,1)S(1)} copy-done((bf16[8,512,512]{2,1,0:T(8,128)(2,1)S(1)}, bf16[8,512,512]{2,1,0:T(8,128)(2,1)}, u32[]{:S(2)}) %copy-start) | copy-done | bytes 4194328
  2.8 0.0 copy-start.1
  2.8 0.7 %copy-done.1 = f32[8,512]{1,0:T(8,128)S(1)} copy-done((f32[8,512]{1,0:T(8,128)S(1)}, f32[8,512]{1,0:T(8,128)}, u32[]{:S(2)}) %copy-start.1) | copy-done | bytes 16408
  3.5 0.0 copy-start.2
  3.5 0.7 %copy-done.2 = f32[1,8]{1,0:T(1,128)S(1)} copy-done((f32[1,8]{1,0:T(1,128)S(1)}, f32[1,8]{1,0:T(1,128)}, u32[]{:S(2)}) %copy-start.2) | copy-done | bytes 56
  4.2 32.5 %shard_map.50 = (f32[4,512]{1,0:T(4,128)S(1)}, f32[8,512]{1,0:T(8,128)S(1)}) custom-call(bf16[8,512,512]{2,1,0:T(8,128)(2,1)S(1)} %copy-done, f32[8,512]{1,0:T(8,128)S(1)} %copy-done.1, f32[1,8]{1,0:T(1,128)S(1)} %copy-done.2), custom_call_target="tpu_custom_call" | custom-call | flops 536870912 | bytes 4194304 | tf_op jit(solution)/shard_map/pallas_call | solution.py:352
  36.7 0.6 %copy.7 = f32[4,512]{1,0:T(4,128)} copy(f32[4,512]{1,0:T(4,128)S(1)} %get-tuple-element.4) | data formatting | bytes 16384
  37.3 0.6 %copy.8 = f32[8,512]{1,0:T(8,128)} copy(f32[8,512]{1,0:T(8,128)S(1)} %get-tuple-element.5) | data formatting | bytes 32768
Async XLA Ops:
  0.6 2.2 %copy-start = (bf16[8,512,512]{2,1,0:T(8,128)(2,1)S(1)}, bf16[8,512,512]{2,1,0:T(8,128)(2,1)}, u32[]{:S(2)}) copy-start(bf16[8,512,512]{2,1,0:T(8,128)(2,1)} %t_ref.1) | copy-start | bytes 12582916
  2.8 0.7 %copy-start.1 = (f32[8,512]{1,0:T(8,128)S(1)}, f32[8,512]{1,0:T(8,128)}, u32[]{:S(2)}) copy-start(f32[8,512]{1,0:T(8,128)} %b_ref.1) | copy-start | bytes 49156
  3.5 0.7 %copy-start.2 = (f32[1,8]{1,0:T(1,128)S(1)}, f32[1,8]{1,0:T(1,128)}, u32[]{:S(2)}) copy-start(f32[1,8]{1,0:T(1,128)} %c_ref.1) | copy-start | bytes 100

commit v2 on v1

--- a/solution.py
+++ b/solution.py
@@ -124,16 +124,35 @@
 
 def inverse(normal):
     rank = normal.shape[0]
-    lane = lax.broadcasted_iota(jnp.int32, normal.shape, 1)
-    sub = lax.broadcasted_iota(jnp.int32, normal.shape, 0)
-    for k in range(rank):
-        col = normal[:, k : k + 1]
-        row = normal[k : k + 1, :]
-        pivot = 1.0 / normal[k : k + 1, k : k + 1]
-        row = jnp.where(lane[0:1] == k, 1.0, row) * pivot
-        rest = jnp.where(lane == k, 0.0, normal) - col * row
-        normal = jnp.where(sub == k, row, rest)
-    return normal
+    blocks = [normal[q * SUBS : (q + 1) * SUBS] for q in range(rank // SUBS)]
+    lane = lax.broadcasted_iota(jnp.int32, (SUBS, LANES), 1)
+    sub = lax.broadcasted_iota(jnp.int32, (SUBS, LANES), 0)
+
+    def column(block, index):
+        return jnp.broadcast_to(block[:, index : index + 1], (SUBS, LANES))
+
+    for q in range(rank // SUBS):
+        first = q * SUBS
+        cols = [[column(block, first + k) for k in range(SUBS)] for block in blocks]
+        rows, inner = blocks[q], cols[q]
+        for k in range(SUBS):
+            col = inner[k]
+            pivot = 1.0 / col[k : k + 1]
+            row = jnp.where(lane[0:1] == first + k, 1.0, rows[k : k + 1]) * pivot
+            rest = jnp.where(lane == first + k, 0.0, rows) - col * row
+            rows = jnp.where(sub == k, row, rest)
+            for m in range(k + 1, SUBS):
+                entry = inner[m][k : k + 1] * pivot
+                inner[m] = jnp.where(sub == k, entry, inner[m] - col * entry)
+        inside = (lane >= first) & (lane < first + SUBS)
+        for p in range(rank // SUBS):
+            if p != q:
+                total = jnp.where(inside, 0.0, blocks[p])
+                for k in range(SUBS):
+                    total = total - cols[p][k] * rows[k : k + 1]
+                blocks[p] = total
+        blocks[q] = rows
+    return jnp.concatenate(blocks, axis=0)
 
 
 def split(values):
@@ -144,8 +163,8 @@
 def kernel(
     n_ia, n_ja, total_i, total_j,
     t_ref, b_ref, c_ref, oa_ref, ob_ref,
-    tv, ball, cst, cja, cia, gb, pbuf, ra, ga, araw, gr, rb, wsc, sq,
-    t_sem, b_s, b_r, cj_s, cj_r, ci_s, ci_r, gb_s, gb_r, ra_s, ra_r, ga_s, ga_r,
+    tv, ball, cin, cst, cja, cia, gb, pbuf, ra, ga, araw, gr, rb, wsc, sq,
+    t_sem, in_sem, b_s, b_r, cj_s, cj_r, ci_s, ci_r, gb_s, gb_r, ra_s, ra_r, ga_s, ga_r,
     gr_s, gr_r, rb_s, rb_r, sq_s, sq_r,
 ):
     a = lax.axis_index("ia")
@@ -164,6 +183,10 @@
     def on_ja(index):
         return (a, index, 0)
 
+    fetch_c = pltpu.make_async_copy(c_ref, cin, in_sem.at[0])
+    fetch_b = pltpu.make_async_copy(b_ref, ball.at[a], in_sem.at[1])
+    fetch_c.start()
+    fetch_b.start()
     loads = []
     for h in range(halves):
         rows = pl.ds(h * part_i, part_i)
@@ -177,9 +200,10 @@
     for step in range(1, n_ja):
         pl.semaphore_signal(barrier, inc=1, device_id=on_ja(lax.rem(j + step, n_ja)), device_id_type=MESH)
     cst[...] = jnp.zeros_like(cst)
-    cst[0:1, 0:steps] = c_ref[...]
+    fetch_c.wait()
+    cst[0:1, 0:steps] = cin[...]
     cja[j] = cst[...]
-    ball[a] = b_ref[...]
+    fetch_b.wait()
     pl.semaphore_wait(barrier, n_ia + n_ja - 2)
 
     sends = []
@@ -194,7 +218,7 @@
         for copy in copies:
             copy.wait_recv()
 
-    b_copies = begin(spread(b_ref, ball, a, n_ia, on_ia, b_s, b_r))
+    b_copies = begin(spread(ball.at[a], ball, a, n_ia, on_ia, b_s, b_r))
     cj_copies = begin(spread(cst, cja, j, n_ja, on_ja, cj_s, cj_r))
     arrived(cj_copies)
     cia[a] = stacked([cja[s, 0:1, :] for s in range(n_ja)], n_ja)
@@ -331,6 +355,7 @@
     scratch = [
         vmem(tensor.shape, tensor.dtype),
         vmem((n_ia, rows_b, width_j), f32),
+        vmem(factor_c.shape, f32),
         vmem((SUBS, LANES), f32),
         vmem((n_ja, SUBS, LANES), f32),
         vmem((n_ia, n_ja, LANES), f32),
@@ -344,6 +369,7 @@
         vmem((n_ia, SUBS, LANES), f32),
         vmem((n_ja, SUBS, LANES), f32),
         dma((halves,)),
+        dma((2,)),
         *ia_sems, *ja_sems, *ia_sems, *ja_sems, *ja_sems, *ja_sems, *ia_sems,
         dma((cuts_j, n_ia)), dma((cuts_j, n_ia)),
         *ja_sems,
@@ -356,15 +382,15 @@
             jax.ShapeDtypeStruct((rows_b, width_j), f32),
         ),
         in_specs=[
-            pl.BlockSpec(memory_space=pl.ANY),
-            pl.BlockSpec(memory_space=pltpu.VMEM),
-            pl.BlockSpec(memory_space=pltpu.VMEM),
+            pl.BlockSpec(memory_space=pltpu.HBM),
+            pl.BlockSpec(memory_space=pltpu.HBM),
+            pl.BlockSpec(memory_space=pltpu.HBM),
         ],
         out_specs=(pl.BlockSpec(memory_space=pltpu.VMEM), pl.BlockSpec(memory_space=pltpu.VMEM)),
         scratch_shapes=scratch,
         cost_estimate=pl.CostEstimate(flops=flops, bytes_accessed=2 * tensor.size, transcendentals=0),
         compiler_params=pltpu.CompilerParams(
-            collective_id=0, has_side_effects=True, vmem_limit_bytes=40 * 2**20
+            collective_id=0, has_side_effects=True, vmem_limit_bytes=24 * 2**20
         ),
     )(tensor, factor_b, factor_c)
 

time: 38.1 us -> 38.2 us (level)
  no operation moved by 1% of the time
where the time goes in v2:
time: 38.2 us; the launch traced here: 37.9 us
  Pallas kernels  32.5 us (85%)
  local copies, waits for them, and re-layouts  4.76 us (12%)
  between operations  0.65 us (2%)
    pallas_call x1, Pallas kernels, fused(): pl.pallas_call(functools.partial(kernel, n_ia, n_ja, width_i * n_ia, widt...  32.5 us
    unnamed x8, local copies, waits for them, and re-layouts  4.76 us

profile of v2, /device:TPU:0, one launch (start us, length us, event | category | flops | bytes accessed | tf_op | source)
XLA Modules:
  0.0 37.9 jit_solution(5529136647376199711)
XLA Ops:
  0.6 0.0 copy-start
  0.6 2.2 %copy-done = bf16[8,512,512]{2,1,0:T(8,128)(2,1)S(1)} copy-done((bf16[8,512,512]{2,1,0:T(8,128)(2,1)S(1)}, bf16[8,512,512]{2,1,0:T(8,128)(2,1)}, u32[]{:S(2)}) %copy-start) | copy-done | bytes 4194328
  2.8 0.0 copy-start.1
  2.8 0.7 %copy-done.1 = f32[8,512]{1,0:T(8,128)S(1)} copy-done((f32[8,512]{1,0:T(8,128)S(1)}, f32[8,512]{1,0:T(8,128)}, u32[]{:S(2)}) %copy-start.1) | copy-done | bytes 16408
  3.5 0.0 copy-start.2
  3.5 0.7 %copy-done.2 = f32[1,8]{1,0:T(1,128)S(1)} copy-done((f32[1,8]{1,0:T(1,128)S(1)}, f32[1,8]{1,0:T(1,128)}, u32[]{:S(2)}) %copy-start.2) | copy-done | bytes 56
  4.2 32.5 %shard_map.50 = (f32[4,512]{1,0:T(4,128)S(1)}, f32[8,512]{1,0:T(8,128)S(1)}) custom-call(bf16[8,512,512]{2,1,0:T(8,128)(2,1)S(1)} %copy-done, f32[8,512]{1,0:T(8,128)S(1)} %copy-done.1, f32[1,8]{1,0:T(1,128)S(1)} %copy-done.2), custom_call_target="tpu_custom_call" | custom-call | flops 536870912 | bytes 4194304 | tf_op jit(solution)/shard_map/pallas_call | solution.py:378
  36.7 0.6 %copy.7 = f32[4,512]{1,0:T(4,128)} copy(f32[4,512]{1,0:T(4,128)S(1)} %get-tuple-element.4) | data formatting | bytes 16384
  37.3 0.6 %copy.8 = f32[8,512]{1,0:T(8,128)} copy(f32[8,512]{1,0:T(8,128)S(1)} %get-tuple-element.5) | data formatting | bytes 32768
Async XLA Ops:
  0.6 2.2 %copy-start = (bf16[8,512,512]{2,1,0:T(8,128)(2,1)S(1)}, bf16[8,512,512]{2,1,0:T(8,128)(2,1)}, u32[]{:S(2)}) copy-start(bf16[8,512,512]{2,1,0:T(8,128)(2,1)} %t_ref.1) | copy-start | bytes 12582916
  2.8 0.7 %copy-start.1 = (f32[8,512]{1,0:T(8,128)S(1)}, f32[8,512]{1,0:T(8,128)}, u32[]{:S(2)}) copy-start(f32[8,512]{1,0:T(8,128)} %b_ref.1) | copy-start | bytes 49156
  3.5 0.7 %copy-start.2 = (f32[1,8]{1,0:T(1,128)S(1)}, f32[1,8]{1,0:T(1,128)}, u32[]{:S(2)}) copy-start(f32[1,8]{1,0:T(1,128)} %c_ref.1) | copy-start | bytes 100

commit v3 on v2

--- a/solution.py
+++ b/solution.py
@@ -105,6 +105,23 @@
     return lax.dot_general(block, other, NT, precision=HIGH, preferred_element_type=jnp.float32)
 
 
+def parts(values, rows):
+    high = values.astype(jnp.bfloat16).astype(jnp.float32)
+    rest = values - high
+    middle = rest.astype(jnp.bfloat16).astype(jnp.float32)
+    return stacked([high, middle, rest - middle], rows)
+
+
+def folded(products, rank):
+    total = products[0:rank] + products[rank : 2 * rank] + products[2 * rank : 3 * rank]
+    return total + pltpu.roll(total, LANES - rank, 1) + pltpu.roll(total, LANES - 2 * rank, 1)
+
+
+def masked(gram):
+    lane = lax.broadcasted_iota(jnp.int32, gram.shape, 1)
+    return jnp.where(lane < gram.shape[0], gram, 0.0)
+
+
 def packed(gram):
     rank = gram.shape[0]
     tile = gram[0:SUBS]
@@ -163,7 +180,7 @@
 def kernel(
     n_ia, n_ja, total_i, total_j,
     t_ref, b_ref, c_ref, oa_ref, ob_ref,
-    tv, ball, cin, cst, cja, cia, gb, pbuf, ra, ga, araw, gr, rb, wsc, sq,
+    tv, ball, cin, cst, cja, cia, gb, pbuf, ra, ga, araw, gr, rb, wsc, sq, prod,
     t_sem, in_sem, b_s, b_r, cj_s, cj_r, ci_s, ci_r, gb_s, gb_r, ra_s, ra_r, ga_s, ga_r,
     gr_s, gr_r, rb_s, rb_r, sq_s, sq_r,
 ):
@@ -218,20 +235,14 @@
         for copy in copies:
             copy.wait_recv()
 
+    cj_copies = begin(spread(cst, cja, j, n_ja, on_ja, cj_s, cj_r))
     b_copies = begin(spread(ball.at[a], ball, a, n_ia, on_ia, b_s, b_r))
-    cj_copies = begin(spread(cst, cja, j, n_ja, on_ja, cj_s, cj_r))
     arrived(cj_copies)
     cia[a] = stacked([cja[s, 0:1, :] for s in range(n_ja)], n_ja)
     ci_copies = begin(spread(cia.at[a], cia, a, n_ia, on_ia, ci_s, ci_r))
     arrived(b_copies)
-    b_all = stacked([ball[s] for s in range(n_ia)], rank)
-    gb[j] = packed(wide_gram(b_all))
-    gb_copies = begin(spread(gb.at[j], gb, j, n_ja, on_ja, gb_s, gb_r))
-    weights = stacked(list(split(b_all)), LANES).T.astype(jnp.bfloat16)
-    arrived(ci_copies)
-    c_all = stacked([cia[s] for s in range(n_ia)], rank)
-    gram_c = wide_gram(c_all)
-    c_rows = stacked([c_all, c_all], LANES).T
+    b_parts = parts(stacked([ball[s] for s in range(n_ia)], rank), LANES)
+    weights = b_parts.T.astype(jnp.bfloat16)
 
     ra_copies = []
     for step in range(1, n_ja):
@@ -246,16 +257,36 @@
                 device_id_type=MESH,
             )
         )
+
+    def product_a(h, k):
+        return jnp.dot(
+            tv[k, h * part_i : (h + 1) * part_i, :], weights, preferred_element_type=jnp.float32
+        )
+
+    loads[0].wait()
+    for k in range(steps):
+        prod[k] = product_a(0, k)
+    gb[j] = packed(
+        masked(
+            folded(
+                jnp.dot(b_parts.astype(jnp.bfloat16), weights, preferred_element_type=jnp.float32),
+                rank,
+            )
+        )
+    )
+    gb_copies = begin(spread(gb.at[j], gb, j, n_ja, on_ja, gb_s, gb_r))
+    arrived(ci_copies)
+    c_all = stacked([cia[s] for s in range(n_ia)], rank)
+    c_rows = stacked([c_all, c_all, c_all], LANES).T
     for h in range(halves):
-        loads[h].wait()
+        if h:
+            loads[h].wait()
         total = jnp.zeros((part_i, LANES), jnp.float32)
         for k in range(steps):
-            product = jnp.dot(
-                tv[k, h * part_i : (h + 1) * part_i, :], weights, preferred_element_type=jnp.float32
-            )
+            product = product_a(h, k) if h else prod[k]
             total = total + product * c_rows[k : k + 1, :]
         total = total.T
-        total = total[0:rank] + total[rank : 2 * rank]
+        total = total[0:rank] + total[rank : 2 * rank] + total[2 * rank : 3 * rank]
         for q in range(groups):
             pbuf[q * halves + h] = total[q * SUBS : (q + 1) * SUBS]
         for step in range(1, n_ja):
@@ -264,6 +295,7 @@
                 ra_copies[step - 1].start()
     sends.extend(ra_copies)
     ra[j] = pbuf[j]
+    gram_c = wide_gram(c_all)
 
     arrived(gb_copies)
     gram_b = unpacked(functools.reduce(jnp.add, [gb[s] for s in range(n_ja)]), rank)
@@ -283,7 +315,9 @@
     )
     raw_a = jnp.dot(solve_a[:, 0:rank], summed, precision=HIGH, preferred_element_type=jnp.float32)
     araw[...] = raw_a
-    gr[a] = packed(wide_gram(raw_a))
+    a_parts = parts(raw_a, LANES).astype(jnp.bfloat16)
+    products = lax.dot_general(a_parts, a_parts, NT, preferred_element_type=jnp.float32)
+    gr[a] = packed(masked(folded(products, rank)))
     gr_copies = begin(spread(gr.at[a], gr, a, n_ia, on_ia, gr_s, gr_r))
 
     rb_copies = []
@@ -368,6 +402,7 @@
         vmem((cuts_j, n_ia, rank, width_j // cuts_j), f32),
         vmem((n_ia, SUBS, LANES), f32),
         vmem((n_ja, SUBS, LANES), f32),
+        vmem((steps, width_i // halves, LANES), f32),
         dma((halves,)),
         dma((2,)),
         *ia_sems, *ja_sems, *ia_sems, *ja_sems, *ja_sems, *ja_sems, *ia_sems,
@@ -390,7 +425,7 @@
         scratch_shapes=scratch,
         cost_estimate=pl.CostEstimate(flops=flops, bytes_accessed=2 * tensor.size, transcendentals=0),
         compiler_params=pltpu.CompilerParams(
-            collective_id=0, has_side_effects=True, vmem_limit_bytes=24 * 2**20
+            collective_id=0, has_side_effects=True, vmem_limit_bytes=56 * 2**20
         ),
     )(tensor, factor_b, factor_c)
 

time: 38.2 us -> 35.8 us (0.937)
  local copies, waits for them, and re-layouts: 4.76 us -> 2.62 us
    unnamed x8 -> x2, local copies, waits for them, and re-layouts: 4.76 us -> 2.62 us
where the time goes in v3:
time: 35.8 us; the launch traced here: 35.4 us
  Pallas kernels  32.2 us (90%)
  local copies, waits for them, and re-layouts  2.62 us (7%)
  between operations  0.64 us (2%)
    pallas_call x1, Pallas kernels, fused(): pl.pallas_call(functools.partial(kernel, n_ia, n_ja, width_i * n_ia, widt...  32.2 us
    unnamed x2, local copies, waits for them, and re-layouts  2.62 us

profile of v3, /device:TPU:0, one launch (start us, length us, event | category | flops | bytes accessed | tf_op | source)
XLA Modules:
  0.0 35.4 jit_solution(6763849528682644892)
XLA Ops:
  0.6 32.2 %shard_map.50 = (f32[4,512]{1,0:T(4,128)}, f32[8,512]{1,0:T(8,128)}) custom-call(bf16[8,512,512]{2,1,0:T(8,128)(2,1)} %t_ref.1, f32[8,512]{1,0:T(8,128)} %b_ref.1, f32[1,8]{1,0:T(1,128)} %c_ref.1), custom_call_target="tpu_custom_call" | custom-call | flops 536870912 | bytes 4194304 | tf_op jit(solution)/shard_map/pallas_call | solution.py:413
  32.8 1.3 %copy.7 = f32[4,512]{1,0:T(4,128)} copy(f32[4,512]{1,0:T(4,128)} %get-tuple-element.4) | data formatting | bytes 16384
  34.1 1.3 %copy.8 = f32[8,512]{1,0:T(8,128)} copy(f32[8,512]{1,0:T(8,128)} %get-tuple-element.5) | data formatting | bytes 32768

commit v4 on v3

--- a/solution.py
+++ b/solution.py
@@ -180,9 +180,9 @@
 def kernel(
     n_ia, n_ja, total_i, total_j,
     t_ref, b_ref, c_ref, oa_ref, ob_ref,
-    tv, ball, cin, cst, cja, cia, gb, pbuf, ra, ga, araw, gr, rb, wsc, sq, prod,
-    t_sem, in_sem, b_s, b_r, cj_s, cj_r, ci_s, ci_r, gb_s, gb_r, ra_s, ra_r, ga_s, ga_r,
-    gr_s, gr_r, rb_s, rb_r, sq_s, sq_r,
+    tv, ball, cin, cs, gb, pbuf, ra, ga, araw, gr, pb, rb, wsc, sq, rs, rf, prod,
+    t_sem, in_sem, b_s, b_r, c_s, c_r, gb_s, gb_r, ra_s, ra_r, ga_s, ga_r,
+    gr_s, gr_r, rb_s, rb_r, sq_s, sq_r, rf_s, rf_r,
 ):
     a = lax.axis_index("ia")
     j = lax.axis_index("ja")
@@ -191,8 +191,15 @@
     groups = rank // SUBS
     halves = n_ja // groups
     part_i = width_i // halves
-    cuts_j = rb.shape[0]
+    cuts_j = 2
     part_j = width_j // cuts_j
+    piece_j = width_j // n_ia
+
+    n_all = n_ia * n_ja
+    mine = a * n_ja + j
+
+    def on_all(index):
+        return (index // n_ja, lax.rem(index, n_ja), 0)
 
     def on_ia(index):
         return (index, j, 0)
@@ -212,16 +219,13 @@
         loads.append(load)
 
     barrier = pltpu.get_barrier_semaphore()
-    for step in range(1, n_ia):
-        pl.semaphore_signal(barrier, inc=1, device_id=on_ia(lax.rem(a + step, n_ia)), device_id_type=MESH)
-    for step in range(1, n_ja):
-        pl.semaphore_signal(barrier, inc=1, device_id=on_ja(lax.rem(j + step, n_ja)), device_id_type=MESH)
-    cst[...] = jnp.zeros_like(cst)
+    for step in range(1, n_all):
+        pl.semaphore_signal(barrier, inc=1, device_id=on_all(lax.rem(mine + step, n_all)), device_id_type=MESH)
     fetch_c.wait()
-    cst[0:1, 0:steps] = cin[...]
-    cja[j] = cst[...]
+    cs[mine] = jnp.zeros((1, LANES), jnp.float32)
+    cs[mine, :, 0:steps] = cin[...]
     fetch_b.wait()
-    pl.semaphore_wait(barrier, n_ia + n_ja - 2)
+    pl.semaphore_wait(barrier, n_all - 1)
 
     sends = []
 
@@ -235,11 +239,8 @@
         for copy in copies:
             copy.wait_recv()
 
-    cj_copies = begin(spread(cst, cja, j, n_ja, on_ja, cj_s, cj_r))
     b_copies = begin(spread(ball.at[a], ball, a, n_ia, on_ia, b_s, b_r))
-    arrived(cj_copies)
-    cia[a] = stacked([cja[s, 0:1, :] for s in range(n_ja)], n_ja)
-    ci_copies = begin(spread(cia.at[a], cia, a, n_ia, on_ia, ci_s, ci_r))
+    c_copies = begin(spread(cs.at[mine], cs, mine, n_all, on_all, c_s, c_r))
     arrived(b_copies)
     b_parts = parts(stacked([ball[s] for s in range(n_ia)], rank), LANES)
     weights = b_parts.T.astype(jnp.bfloat16)
@@ -275,8 +276,8 @@
         )
     )
     gb_copies = begin(spread(gb.at[j], gb, j, n_ja, on_ja, gb_s, gb_r))
-    arrived(ci_copies)
-    c_all = stacked([cia[s] for s in range(n_ia)], rank)
+    arrived(c_copies)
+    c_all = stacked([cs[s] for s in range(n_all)], rank)
     c_rows = stacked([c_all, c_all, c_all], LANES).T
     for h in range(halves):
         if h:
@@ -321,6 +322,18 @@
     gr_copies = begin(spread(gr.at[a], gr, a, n_ia, on_ia, gr_s, gr_r))
 
     rb_copies = []
+    for step in range(1, n_ia):
+        peer = lax.rem(a + step, n_ia)
+        rb_copies.append(
+            pltpu.make_async_remote_copy(
+                src_ref=pb.at[peer],
+                dst_ref=rb.at[a],
+                send_sem=rb_s.at[step],
+                recv_sem=rb_r.at[step],
+                device_id=on_ia(peer),
+                device_id_type=MESH,
+            )
+        )
     pieces = []
     for k in range(steps):
         pieces.append(jnp.concatenate(split(raw_a * c_cols[k]), axis=0).astype(jnp.bfloat16))
@@ -330,10 +343,15 @@
             total = total + jnp.dot(
                 pieces[k], tv[k, :, h * part_j : (h + 1) * part_j], preferred_element_type=jnp.float32
             )
-        rb[h, a] = total[0:rank] + total[rank : 2 * rank]
-        rb_copies.extend(
-            begin(spread(rb.at[h, a], rb.at[h], a, n_ia, on_ia, rb_s.at[h], rb_r.at[h]))
-        )
+        total = total[0:rank] + total[rank : 2 * rank]
+        for m in range(n_ia // cuts_j):
+            pb[h * (n_ia // cuts_j) + m] = total[:, m * piece_j : (m + 1) * piece_j]
+        for step in range(1, n_ia):
+            @pl.when(lax.rem(a + step, n_ia) // (n_ia // cuts_j) == h)
+            def _():
+                rb_copies[step - 1].start()
+    sends.extend(rb_copies)
+    rb[a] = pb[a]
 
     arrived(gr_copies)
     gram_a = unpacked(functools.reduce(jnp.add, [gr[s] for s in range(n_ia)]), rank)
@@ -343,8 +361,6 @@
     scale_col = 1.0 / jnp.sqrt(jnp.sum(squares, axis=1, keepdims=True) / total_i + EPS)
     scale_row = 1.0 / jnp.sqrt(jnp.sum(squares, axis=0, keepdims=True) / total_i + EPS)
     solve_b = inverse(gram_a * scale_col * scale_row * gram_c) * scale_row
-    for q in range(n_ia):
-        wsc[q] = solve_b[q * SUBS : (q + 1) * SUBS]
     new_a = araw[...] * scale_col
     for q in range(groups):
         araw[q * SUBS : (q + 1) * SUBS] = new_a[q * SUBS : (q + 1) * SUBS]
@@ -353,24 +369,55 @@
         @pl.when(j == p)
         def _():
             oa_ref[...] = araw[p * height : (p + 1) * height, :]
-    solve_own = wsc[a][:, 0:rank]
 
     arrived(rb_copies)
-    raw_b = []
-    for h in range(cuts_j):
-        summed_b = functools.reduce(jnp.add, [rb[h, s] for s in range(n_ia)])
-        raw_b.append(
-            jnp.dot(solve_own, summed_b, precision=HIGH, preferred_element_type=jnp.float32)
+    summed_b = functools.reduce(jnp.add, [rb[s] for s in range(n_ia)])
+    raw_b = jnp.dot(solve_b[:, 0:rank], summed_b, precision=HIGH, preferred_element_type=jnp.float32)
+    sums = jnp.sum(raw_b * raw_b, axis=1, keepdims=True)
+    sq[mine] = jnp.sum(jnp.where(lane == sub, sums, 0.0), axis=0, keepdims=True)
+    for q in range(n_ia):
+        rs[q] = raw_b[q * SUBS : (q + 1) * SUBS]
+    rf[a] = rs[a]
+    sq_copies = spread(sq.at[mine], sq, mine, n_all, on_all, sq_s, sq_r)
+    rf_copies = []
+    for step in range(1, n_ia):
+        peer = lax.rem(a + step, n_ia)
+        rf_copies.append(
+            pltpu.make_async_remote_copy(
+                src_ref=rs.at[peer],
+                dst_ref=rf.at[a],
+                send_sem=rf_s.at[step],
+                recv_sem=rf_r.at[step],
+                device_id=on_ia(peer),
+                device_id_type=MESH,
+            )
         )
-    raw_b = jnp.concatenate(raw_b, axis=1)
-    sq[j] = jnp.broadcast_to(jnp.sum(raw_b * raw_b, axis=1, keepdims=True), (SUBS, LANES))
-    sq_copies = begin(spread(sq.at[j], sq, j, n_ja, on_ja, sq_s, sq_r))
+    begin(rf_copies)
+    begin(sq_copies)
+    arrived(rf_copies)
     arrived(sq_copies)
-    squares_b = functools.reduce(jnp.add, [sq[s] for s in range(n_ja)])[:, 0:1]
-    ob_ref[...] = raw_b / jnp.sqrt(squares_b / total_j + EPS)
+    squares_b = functools.reduce(jnp.add, [sq[s] for s in range(n_all)])
+    total_b = jnp.sum(jnp.where(lane == sub, squares_b, 0.0), axis=1, keepdims=True)
+    scale_b = jnp.broadcast_to(1.0 / jnp.sqrt(total_b / total_j + EPS), (rank, LANES))
+    for q in range(n_ia):
+        wsc[q] = scale_b[q * SUBS : (q + 1) * SUBS]
+    own = wsc[a]
+    for q in range(n_ia):
+        ob_ref[:, q * piece_j : (q + 1) * piece_j] = rf[q] * own
 
     for copy in sends:
         copy.wait_send()
+
+
+def write_out(a_ref, b_ref, oa_ref, ob_ref, sems):
+    copies = [
+        pltpu.make_async_copy(a_ref, oa_ref, sems.at[0]),
+        pltpu.make_async_copy(b_ref, ob_ref, sems.at[1]),
+    ]
+    for copy in copies:
+        copy.start()
+    for copy in copies:
+        copy.wait()
 
 
 def fused(tensor, factor_b, factor_c):
@@ -380,37 +427,36 @@
     rows_b = factor_b.shape[0]
     rank = rows_b * n_ia
     halves = n_ja // (rank // SUBS)
-    cuts_j = 2
     f32 = jnp.float32
     vmem = pltpu.VMEM
     dma = pltpu.SemaphoreType.DMA
     ja_sems = [dma((n_ja,)), dma((n_ja,))]
     ia_sems = [dma((n_ia,)), dma((n_ia,))]
+    all_sems = [dma((n_ia * n_ja,)), dma((n_ia * n_ja,))]
     scratch = [
         vmem(tensor.shape, tensor.dtype),
         vmem((n_ia, rows_b, width_j), f32),
         vmem(factor_c.shape, f32),
-        vmem((SUBS, LANES), f32),
-        vmem((n_ja, SUBS, LANES), f32),
-        vmem((n_ia, n_ja, LANES), f32),
+        vmem((n_ia * n_ja, 1, LANES), f32),
         vmem((n_ja, SUBS, LANES), f32),
         vmem((n_ja, SUBS, width_i // halves), f32),
         vmem((n_ja, SUBS, width_i // halves), f32),
         vmem((n_ja, SUBS, width_i // halves), f32),
         vmem((rank, width_i), f32),
         vmem((n_ia, SUBS, LANES), f32),
-        vmem((cuts_j, n_ia, rank, width_j // cuts_j), f32),
+        vmem((n_ia, rank, width_j // n_ia), f32),
+        vmem((n_ia, rank, width_j // n_ia), f32),
         vmem((n_ia, SUBS, LANES), f32),
-        vmem((n_ja, SUBS, LANES), f32),
+        vmem((n_ia * n_ja, 1, LANES), f32),
+        vmem((n_ia, SUBS, width_j // n_ia), f32),
+        vmem((n_ia, SUBS, width_j // n_ia), f32),
         vmem((steps, width_i // halves, LANES), f32),
         dma((halves,)),
         dma((2,)),
-        *ia_sems, *ja_sems, *ia_sems, *ja_sems, *ja_sems, *ja_sems, *ia_sems,
-        dma((cuts_j, n_ia)), dma((cuts_j, n_ia)),
-        *ja_sems,
+        *ia_sems, *all_sems, *ja_sems, *ja_sems, *ja_sems, *ia_sems, *ia_sems, *all_sems, *ia_sems,
     ]
     flops = 8 * rank * tensor.size
-    return pl.pallas_call(
+    results = pl.pallas_call(
         functools.partial(kernel, n_ia, n_ja, width_i * n_ia, width_j * n_ja),
         out_shape=(
             jax.ShapeDtypeStruct((rank // n_ja, width_i), f32),
@@ -428,11 +474,20 @@
             collective_id=0, has_side_effects=True, vmem_limit_bytes=56 * 2**20
         ),
     )(tensor, factor_b, factor_c)
+    anywhere = pl.BlockSpec(memory_space=pl.ANY)
+    return pl.pallas_call(
+        write_out,
+        out_shape=tuple(jax.ShapeDtypeStruct(r.shape, r.dtype) for r in results),
+        in_specs=[anywhere, anywhere],
+        out_specs=(anywhere, anywhere),
+        scratch_shapes=[dma((2,))],
+        compiler_params=pltpu.CompilerParams(vmem_limit_bytes=56 * 2**20),
+    )(*results)
 
 
 def fits(mesh):
     n_ia, n_ja, n_ka = (mesh.shape[name] for name in ("ia", "ja", "ka"))
-    return n_ka == 1 and n_ia * SUBS == 32 and n_ja % n_ia == 0 and n_ja <= SUBS
+    return n_ka == 1 and n_ia * SUBS == 32 and n_ja == 2 * n_ia
 
 
 def solution(mesh):

time: 35.8 us -> 34.3 us (0.958)
  local copies, waits for them, and re-layouts: 2.62 us -> 0 us
  Pallas kernels: 32.2 us -> 33.5 us
    unnamed x2 -> x0, local copies, waits for them, and re-layouts: 2.62 us -> none
    pallas_call x0 -> x1, Pallas kernels: none -> 1.87 us  [fused(): pl.pallas_call(write_out, out_shape=tuple((jax.ShapeDtypeStruct(r.shape,...]
    pallas_call x1, Pallas kernels: 32.2 us -> 31.7 us  [fused(): pl.pallas_call(functools.partial(kernel, n_ia, n_ja, width_i * n_ia, widt...]
where the time goes in v4:
time: 34.3 us; the launch traced here: 34.2 us
  Pallas kernels  33.5 us (98%)
  between operations  0.64 us (2%)
    pallas_call x1, Pallas kernels, fused(): pl.pallas_call(functools.partial(kernel, n_ia, n_ja, width_i * n_ia, widt...  31.7 us
    pallas_call x1, Pallas kernels, fused(): pl.pallas_call(write_out, out_shape=tuple((jax.ShapeDtypeStruct(r.shape,...  1.87 us

profile of v4, /device:TPU:0, one launch (start us, length us, event | category | flops | bytes accessed | tf_op | source)
XLA Modules:
  0.0 34.2 jit_solution(6157853390218084826)
XLA Ops:
  0.6 31.7 %shard_map.50 = (f32[4,512]{1,0:T(4,128)}, f32[8,512]{1,0:T(8,128)}) custom-call(bf16[8,512,512]{2,1,0:T(8,128)(2,1)} %t_ref.1, f32[8,512]{1,0:T(8,128)} %b_ref.1, f32[1,8]{1,0:T(1,128)} %c_ref.1), custom_call_target="tpu_custom_call" | custom-call | flops 536870912 | bytes 4194304 | tf_op jit(solution)/shard_map/pallas_call | solution.py:459
  32.3 1.9 %shard_map.51 = (f32[4,512]{1,0:T(4,128)}, f32[8,512]{1,0:T(8,128)}) custom-call(f32[4,512]{1,0:T(4,128)} %get-tuple-element.4.a_ref, f32[8,512]{1,0:T(8,128)} %get-tuple-element.5.b_ref), custom_call_target="tpu_custom_call" | custom-call | tf_op jit(solution)/shard_map/pallas_call | solution.py:478

commit v5 on v4

--- a/solution.py
+++ b/solution.py
@@ -77,20 +77,24 @@
 NT = (((1,), (1,)), ((), ()))
 
 
-def spread(src, dst, me, count, device, send, recv):
+def spread(src, dst, me, peers, send, recv):
     copies = []
-    for step in range(1, count):
+    for step, peer in enumerate(peers, 1):
         copies.append(
             pltpu.make_async_remote_copy(
                 src_ref=src,
                 dst_ref=dst.at[me],
                 send_sem=send.at[step],
                 recv_sem=recv.at[step],
-                device_id=device(lax.rem(me + step, count)),
+                device_id=peer,
                 device_id_type=MESH,
             )
         )
     return copies
+
+
+def ring(me, count):
+    return [me] + [jnp.where(me + step >= count, me + step - count, me + step) for step in range(1, count)]
 
 
 def stacked(pieces, rows):
@@ -120,6 +124,27 @@
 def masked(gram):
     lane = lax.broadcasted_iota(jnp.int32, gram.shape, 1)
     return jnp.where(lane < gram.shape[0], gram, 0.0)
+
+
+def applied(solver, values):
+    rank = solver.shape[0]
+    s_parts = parts(solver, 3 * rank)
+    high, middle, low = (s_parts[p * rank : (p + 1) * rank] for p in range(3))
+    left = jnp.concatenate(
+        [
+            high + pltpu.roll(high, rank, 1) + pltpu.roll(high, 2 * rank, 1) + pltpu.roll(middle, 3 * rank, 1),
+            middle + pltpu.roll(low, rank, 1),
+        ],
+        axis=1,
+    ).astype(jnp.bfloat16)
+    v_high, v_middle, v_low = (
+        p.astype(jnp.bfloat16) for p in jnp.split(parts(values, 3 * rank), 3, axis=0)
+    )
+    blank = jnp.zeros_like(v_high)
+    right = jnp.concatenate(
+        [v_high, v_middle, v_low, v_high, v_middle, v_high, blank, blank], axis=0
+    )
+    return jnp.dot(left, right, preferred_element_type=jnp.float32)
 
 
 def packed(gram):
@@ -198,14 +223,12 @@
     n_all = n_ia * n_ja
     mine = a * n_ja + j
 
-    def on_all(index):
-        return (index // n_ja, lax.rem(index, n_ja), 0)
-
-    def on_ia(index):
-        return (index, j, 0)
-
-    def on_ja(index):
-        return (a, index, 0)
+    ring_a, ring_j = ring(a, n_ia), ring(j, n_ja)
+    zero = jnp.int32(0)
+    peers_ia = [(p, j, zero) for p in ring_a[1:]]
+    peers_ja = [(a, q, zero) for q in ring_j[1:]]
+    peers_all = [(p, q, zero) for q in reversed(ring_j) for p in ring_a][:-n_ia]
+    peers_all = peers_all + peers_ia
 
     fetch_c = pltpu.make_async_copy(c_ref, cin, in_sem.at[0])
     fetch_b = pltpu.make_async_copy(b_ref, ball.at[a], in_sem.at[1])
@@ -219,8 +242,8 @@
         loads.append(load)
 
     barrier = pltpu.get_barrier_semaphore()
-    for step in range(1, n_all):
-        pl.semaphore_signal(barrier, inc=1, device_id=on_all(lax.rem(mine + step, n_all)), device_id_type=MESH)
+    for peer in peers_all:
+        pl.semaphore_signal(barrier, inc=1, device_id=peer, device_id_type=MESH)
     fetch_c.wait()
     cs[mine] = jnp.zeros((1, LANES), jnp.float32)
     cs[mine, :, 0:steps] = cin[...]
@@ -239,22 +262,22 @@
         for copy in copies:
             copy.wait_recv()
 
-    b_copies = begin(spread(ball.at[a], ball, a, n_ia, on_ia, b_s, b_r))
-    c_copies = begin(spread(cs.at[mine], cs, mine, n_all, on_all, c_s, c_r))
+    b_copies = begin(spread(ball.at[a], ball, a, peers_ia, b_s, b_r))
+    c_copies = begin(spread(cs.at[mine], cs, mine, peers_all, c_s, c_r))
     arrived(b_copies)
     b_parts = parts(stacked([ball[s] for s in range(n_ia)], rank), LANES)
     weights = b_parts.T.astype(jnp.bfloat16)
 
     ra_copies = []
     for step in range(1, n_ja):
-        peer = lax.rem(j + step, n_ja)
+        peer = ring_j[step]
         ra_copies.append(
             pltpu.make_async_remote_copy(
                 src_ref=pbuf.at[peer],
                 dst_ref=ra.at[j],
                 send_sem=ra_s.at[step],
                 recv_sem=ra_r.at[step],
-                device_id=on_ja(peer),
+                device_id=(a, peer, zero),
                 device_id_type=MESH,
             )
         )
@@ -275,7 +298,7 @@
             )
         )
     )
-    gb_copies = begin(spread(gb.at[j], gb, j, n_ja, on_ja, gb_s, gb_r))
+    gb_copies = begin(spread(gb.at[j], gb, j, peers_ja, gb_s, gb_r))
     arrived(c_copies)
     c_all = stacked([cs[s] for s in range(n_all)], rank)
     c_rows = stacked([c_all, c_all, c_all], LANES).T
@@ -291,7 +314,7 @@
         for q in range(groups):
             pbuf[q * halves + h] = total[q * SUBS : (q + 1) * SUBS]
         for step in range(1, n_ja):
-            @pl.when(lax.rem(j + step, halves) == h)
+            @pl.when(lax.rem(ring_j[step], halves) == h)
             def _():
                 ra_copies[step - 1].start()
     sends.extend(ra_copies)
@@ -304,7 +327,7 @@
 
     arrived(ra_copies)
     ga[j] = functools.reduce(jnp.add, [ra[s] for s in range(n_ja)])
-    ga_copies = begin(spread(ga.at[j], ga, j, n_ja, on_ja, ga_s, ga_r))
+    ga_copies = begin(spread(ga.at[j], ga, j, peers_ja, ga_s, ga_r))
     c_cols = [c_all[:, k : k + 1] for k in range(steps)]
     arrived(ga_copies)
     summed = stacked(
@@ -314,23 +337,23 @@
         ],
         rank,
     )
-    raw_a = jnp.dot(solve_a[:, 0:rank], summed, precision=HIGH, preferred_element_type=jnp.float32)
+    raw_a = applied(solve_a, summed)
     araw[...] = raw_a
     a_parts = parts(raw_a, LANES).astype(jnp.bfloat16)
     products = lax.dot_general(a_parts, a_parts, NT, preferred_element_type=jnp.float32)
     gr[a] = packed(masked(folded(products, rank)))
-    gr_copies = begin(spread(gr.at[a], gr, a, n_ia, on_ia, gr_s, gr_r))
+    gr_copies = begin(spread(gr.at[a], gr, a, peers_ia, gr_s, gr_r))
 
     rb_copies = []
     for step in range(1, n_ia):
-        peer = lax.rem(a + step, n_ia)
+        peer = ring_a[step]
         rb_copies.append(
             pltpu.make_async_remote_copy(
                 src_ref=pb.at[peer],
                 dst_ref=rb.at[a],
                 send_sem=rb_s.at[step],
                 recv_sem=rb_r.at[step],
-                device_id=on_ia(peer),
+                device_id=(peer, j, zero),
                 device_id_type=MESH,
             )
         )
@@ -347,7 +370,7 @@
         for m in range(n_ia // cuts_j):
             pb[h * (n_ia // cuts_j) + m] = total[:, m * piece_j : (m + 1) * piece_j]
         for step in range(1, n_ia):
-            @pl.when(lax.rem(a + step, n_ia) // (n_ia // cuts_j) == h)
+            @pl.when(ring_a[step] // (n_ia // cuts_j) == h)
             def _():
                 rb_copies[step - 1].start()
     sends.extend(rb_copies)
@@ -372,23 +395,23 @@
 
     arrived(rb_copies)
     summed_b = functools.reduce(jnp.add, [rb[s] for s in range(n_ia)])
-    raw_b = jnp.dot(solve_b[:, 0:rank], summed_b, precision=HIGH, preferred_element_type=jnp.float32)
+    raw_b = applied(solve_b, summed_b)
     sums = jnp.sum(raw_b * raw_b, axis=1, keepdims=True)
     sq[mine] = jnp.sum(jnp.where(lane == sub, sums, 0.0), axis=0, keepdims=True)
     for q in range(n_ia):
         rs[q] = raw_b[q * SUBS : (q + 1) * SUBS]
     rf[a] = rs[a]
-    sq_copies = spread(sq.at[mine], sq, mine, n_all, on_all, sq_s, sq_r)
+    sq_copies = spread(sq.at[mine], sq, mine, peers_all, sq_s, sq_r)
     rf_copies = []
     for step in range(1, n_ia):
-        peer = lax.rem(a + step, n_ia)
+        peer = ring_a[step]
         rf_copies.append(
             pltpu.make_async_remote_copy(
                 src_ref=rs.at[peer],
                 dst_ref=rf.at[a],
                 send_sem=rf_s.at[step],
                 recv_sem=rf_r.at[step],
-                device_id=on_ia(peer),
+                device_id=(peer, j, zero),
                 device_id_type=MESH,
             )
         )

time: 34.3 us -> 34.3 us (level)
  no operation moved by 1% of the time
where the time goes in v5:
time: 34.3 us; the launch traced here: 34.2 us
  Pallas kernels  33.6 us (98%)
  between operations  0.64 us (2%)
    pallas_call x1, Pallas kernels, fused(): pl.pallas_call(functools.partial(kernel, n_ia, n_ja, width_i * n_ia, widt...  31.7 us
    pallas_call x1, Pallas kernels, fused(): pl.pallas_call(write_out, out_shape=tuple((jax.ShapeDtypeStruct(r.shape,...  1.87 us

profile of v5, /device:TPU:0, one launch (start us, length us, event | category | flops | bytes accessed | tf_op | source)
XLA Modules:
  0.0 34.2 jit_solution(275800567803281849)
XLA Ops:
  0.6 31.7 %shard_map.50 = (f32[4,512]{1,0:T(4,128)}, f32[8,512]{1,0:T(8,128)}) custom-call(bf16[8,512,512]{2,1,0:T(8,128)(2,1)} %t_ref.1, f32[8,512]{1,0:T(8,128)} %b_ref.1, f32[1,8]{1,0:T(1,128)} %c_ref.1), custom_call_target="tpu_custom_call" | custom-call | flops 536870912 | bytes 4194304 | tf_op jit(solution)/shard_map/pallas_call | solution.py:482
  32.3 1.9 %shard_map.51 = (f32[4,512]{1,0:T(4,128)}, f32[8,512]{1,0:T(8,128)}) custom-call(f32[4,512]{1,0:T(4,128)} %get-tuple-element.4.a_ref, f32[8,512]{1,0:T(8,128)} %get-tuple-element.5.b_ref), custom_call_target="tpu_custom_call" | custom-call | tf_op jit(solution)/shard_map/pallas_call | solution.py:501

commit v6 on v5

--- a/solution.py
+++ b/solution.py
@@ -216,8 +216,6 @@
     groups = rank // SUBS
     halves = n_ja // groups
     part_i = width_i // halves
-    cuts_j = 2
-    part_j = width_j // cuts_j
     piece_j = width_j // n_ia
 
     n_all = n_ia * n_ja
@@ -235,9 +233,8 @@
     fetch_c.start()
     fetch_b.start()
     loads = []
-    for h in range(halves):
-        rows = pl.ds(h * part_i, part_i)
-        load = pltpu.make_async_copy(t_ref.at[:, rows], tv.at[:, rows], t_sem.at[h])
+    for k in range(steps):
+        load = pltpu.make_async_copy(t_ref.at[k], tv.at[k], t_sem.at[k])
         load.start()
         loads.append(load)
 
@@ -282,14 +279,11 @@
             )
         )
 
-    def product_a(h, k):
-        return jnp.dot(
-            tv[k, h * part_i : (h + 1) * part_i, :], weights, preferred_element_type=jnp.float32
-        )
-
-    loads[0].wait()
-    for k in range(steps):
-        prod[k] = product_a(0, k)
+    for load in loads:
+        load.wait()
+    prod[...] = jnp.dot(
+        tv[...].reshape(steps * width_i, width_j), weights, preferred_element_type=jnp.float32
+    ).reshape(prod.shape)
     gb[j] = packed(
         masked(
             folded(
@@ -303,12 +297,9 @@
     c_all = stacked([cs[s] for s in range(n_all)], rank)
     c_rows = stacked([c_all, c_all, c_all], LANES).T
     for h in range(halves):
-        if h:
-            loads[h].wait()
         total = jnp.zeros((part_i, LANES), jnp.float32)
         for k in range(steps):
-            product = product_a(h, k) if h else prod[k]
-            total = total + product * c_rows[k : k + 1, :]
+            total = total + prod[k, h * part_i : (h + 1) * part_i, :] * c_rows[k : k + 1, :]
         total = total.T
         total = total[0:rank] + total[rank : 2 * rank] + total[2 * rank : 3 * rank]
         for q in range(groups):
@@ -360,19 +351,16 @@
     pieces = []
     for k in range(steps):
         pieces.append(jnp.concatenate(split(raw_a * c_cols[k]), axis=0).astype(jnp.bfloat16))
-    for h in range(cuts_j):
-        total = jnp.zeros((2 * rank, part_j), jnp.float32)
-        for k in range(steps):
-            total = total + jnp.dot(
-                pieces[k], tv[k, :, h * part_j : (h + 1) * part_j], preferred_element_type=jnp.float32
-            )
-        total = total[0:rank] + total[rank : 2 * rank]
-        for m in range(n_ia // cuts_j):
-            pb[h * (n_ia // cuts_j) + m] = total[:, m * piece_j : (m + 1) * piece_j]
-        for step in range(1, n_ia):
-            @pl.when(ring_a[step] // (n_ia // cuts_j) == h)
-            def _():
-                rb_copies[step - 1].start()
+    total = jnp.dot(
+        jnp.concatenate(pieces, axis=1),
+        tv[...].reshape(steps * width_i, width_j),
+        preferred_element_type=jnp.float32,
+    )
+    total = total[0:rank] + total[rank : 2 * rank]
+    for p in range(n_ia):
+        pb[p] = total[:, p * piece_j : (p + 1) * piece_j]
+    for copy in rb_copies:
+        copy.start()
     sends.extend(rb_copies)
     rb[a] = pb[a]
 
@@ -473,8 +461,8 @@
         vmem((n_ia * n_ja, 1, LANES), f32),
         vmem((n_ia, SUBS, width_j // n_ia), f32),
         vmem((n_ia, SUBS, width_j // n_ia), f32),
-        vmem((steps, width_i // halves, LANES), f32),
-        dma((halves,)),
+        vmem((steps, width_i, LANES), f32),
+        dma((steps,)),
         dma((2,)),
         *ia_sems, *all_sems, *ja_sems, *ja_sems, *ja_sems, *ia_sems, *ia_sems, *all_sems, *ia_sems,
     ]

time: 34.3 us -> 35.2 us (1.026)
  Pallas kernels: 33.6 us -> 34.4 us
    pallas_call x1, Pallas kernels: 31.7 us -> 32.6 us  [fused(): pl.pallas_call(functools.partial(kernel, n_ia, n_ja, width_i * n_ia, widt...]
where the time goes in v6:
time: 35.2 us; the launch traced here: 35.1 us
  Pallas kernels  34.4 us (98%)
  between operations  0.64 us (2%)
    pallas_call x1, Pallas kernels, fused(): pl.pallas_call(functools.partial(kernel, n_ia, n_ja, width_i * n_ia, widt...  32.6 us
    pallas_call x1, Pallas kernels, fused(): pl.pallas_call(write_out, out_shape=tuple((jax.ShapeDtypeStruct(r.shape,...  1.87 us

profile of v6, /device:TPU:0, one launch (start us, length us, event | category | flops | bytes accessed | tf_op | source)
XLA Modules:
  0.0 35.1 jit_solution(5193766914161349688)
XLA Ops:
  0.6 32.6 %shard_map.50 = (f32[4,512]{1,0:T(4,128)}, f32[8,512]{1,0:T(8,128)}) custom-call(bf16[8,512,512]{2,1,0:T(8,128)(2,1)} %t_ref.1, f32[8,512]{1,0:T(8,128)} %b_ref.1, f32[1,8]{1,0:T(1,128)} %c_ref.1), custom_call_target="tpu_custom_call" | custom-call | flops 536870912 | bytes 4194304 | tf_op jit(solution)/shard_map/pallas_call | solution.py:470
  33.2 1.9 %shard_map.51 = (f32[4,512]{1,0:T(4,128)}, f32[8,512]{1,0:T(8,128)}) custom-call(f32[4,512]{1,0:T(4,128)} %get-tuple-element.4.a_ref, f32[8,512]{1,0:T(8,128)} %get-tuple-element.5.b_ref), custom_call_target="tpu_custom_call" | custom-call | tf_op jit(solution)/shard_map/pallas_call | solution.py:489

commit v7 on v5

--- a/solution.py
+++ b/solution.py
@@ -329,20 +329,6 @@
     ga[j] = functools.reduce(jnp.add, [ra[s] for s in range(n_ja)])
     ga_copies = begin(spread(ga.at[j], ga, j, peers_ja, ga_s, ga_r))
     c_cols = [c_all[:, k : k + 1] for k in range(steps)]
-    arrived(ga_copies)
-    summed = stacked(
-        [
-            jnp.concatenate([ga[q * halves + h] for h in range(halves)], axis=1)
-            for q in range(groups)
-        ],
-        rank,
-    )
-    raw_a = applied(solve_a, summed)
-    araw[...] = raw_a
-    a_parts = parts(raw_a, LANES).astype(jnp.bfloat16)
-    products = lax.dot_general(a_parts, a_parts, NT, preferred_element_type=jnp.float32)
-    gr[a] = packed(masked(folded(products, rank)))
-    gr_copies = begin(spread(gr.at[a], gr, a, peers_ia, gr_s, gr_r))
 
     rb_copies = []
     for step in range(1, n_ia):
@@ -357,20 +343,45 @@
                 device_id_type=MESH,
             )
         )
-    pieces = []
-    for k in range(steps):
-        pieces.append(jnp.concatenate(split(raw_a * c_cols[k]), axis=0).astype(jnp.bfloat16))
-    for h in range(cuts_j):
-        total = jnp.zeros((2 * rank, part_j), jnp.float32)
+
+    total = None
+    products = None
+    for h in range(halves):
+        for step in range(1, n_ja):
+            @pl.when(lax.rem(ring_j[n_ja - step], halves) == h)
+            def _():
+                ga_copies[step - 1].wait_recv()
+        summed = stacked([ga[q * halves + h] for q in range(groups)], rank)
+        raw_a = applied(solve_a, summed)
+        cut_i = slice(h * part_i, (h + 1) * part_i)
+        araw[:, cut_i] = raw_a
+        a_parts = parts(raw_a, LANES).astype(jnp.bfloat16)
+        block = lax.dot_general(a_parts, a_parts, NT, preferred_element_type=jnp.float32)
+        products = block if products is None else products + block
+        if h == halves - 1:
+            gr[a] = packed(masked(folded(products, rank)))
+            gr_copies = begin(spread(gr.at[a], gr, a, peers_ia, gr_s, gr_r))
+        pieces = [
+            jnp.concatenate(split(raw_a * c_cols[k]), axis=0).astype(jnp.bfloat16)
+            for k in range(steps)
+        ]
+        if h < halves - 1:
+            for k in range(steps):
+                block = jnp.dot(pieces[k], tv[k, cut_i, :], preferred_element_type=jnp.float32)
+                total = block if total is None else total + block
+    for m in range(cuts_j):
+        cut_j = slice(m * part_j, (m + 1) * part_j)
+        done = total[:, cut_j]
         for k in range(steps):
-            total = total + jnp.dot(
-                pieces[k], tv[k, :, h * part_j : (h + 1) * part_j], preferred_element_type=jnp.float32
+            done = done + jnp.dot(
+                pieces[k], tv[k, cut_i, cut_j], preferred_element_type=jnp.float32
             )
-        total = total[0:rank] + total[rank : 2 * rank]
-        for m in range(n_ia // cuts_j):
-            pb[h * (n_ia // cuts_j) + m] = total[:, m * piece_j : (m + 1) * piece_j]
+        done = done[0:rank] + done[rank : 2 * rank]
+        per_cut = n_ia // cuts_j
+        for p in range(per_cut):
+            pb[m * per_cut + p] = done[:, p * piece_j : (p + 1) * piece_j]
         for step in range(1, n_ia):
-            @pl.when(ring_a[step] // (n_ia // cuts_j) == h)
+            @pl.when(ring_a[step] // per_cut == m)
             def _():
                 rb_copies[step - 1].start()
     sends.extend(rb_copies)

time: 34.3 us -> 34.8 us (1.015)
  Pallas kernels: 33.6 us -> 34 us
    pallas_call x1, Pallas kernels: 31.7 us -> 32.1 us  [fused(): pl.pallas_call(functools.partial(kernel, n_ia, n_ja, width_i * n_ia, widt...]
where the time goes in v7:
time: 34.8 us; the launch traced here: 34.6 us
  Pallas kernels  34 us (98%)
  between operations  0.64 us (2%)
    pallas_call x1, Pallas kernels, fused(): pl.pallas_call(functools.partial(kernel, n_ia, n_ja, width_i * n_ia, widt...  32.1 us
    pallas_call x1, Pallas kernels, fused(): pl.pallas_call(write_out, out_shape=tuple((jax.ShapeDtypeStruct(r.shape,...  1.87 us

profile of v7, /device:TPU:0, one launch (start us, length us, event | category | flops | bytes accessed | tf_op | source)
XLA Modules:
  0.0 34.6 jit_solution(11158895704067890385)
XLA Ops:
  0.6 32.1 %shard_map.50 = (f32[4,512]{1,0:T(4,128)}, f32[8,512]{1,0:T(8,128)}) custom-call(bf16[8,512,512]{2,1,0:T(8,128)(2,1)} %t_ref.1, f32[8,512]{1,0:T(8,128)} %b_ref.1, f32[1,8]{1,0:T(1,128)} %c_ref.1), custom_call_target="tpu_custom_call" | custom-call | flops 536870912 | bytes 4194304 | tf_op jit(solution)/shard_map/pallas_call | solution.py:493
  32.8 1.9 %shard_map.51 = (f32[4,512]{1,0:T(4,128)}, f32[8,512]{1,0:T(8,128)}) custom-call(f32[4,512]{1,0:T(4,128)} %get-tuple-element.4.a_ref, f32[8,512]{1,0:T(8,128)} %get-tuple-element.5.b_ref), custom_call_target="tpu_custom_call" | custom-call | tf_op jit(solution)/shard_map/pallas_call | solution.py:512

commit v8 on v5

--- a/solution.py
+++ b/solution.py
@@ -164,6 +164,12 @@
     return jnp.concatenate(groups, axis=0)
 
 
+def reciprocal(value):
+    guess = pl.reciprocal(value, approx=True)
+    guess = guess * (2.0 - value * guess)
+    return guess * (2.0 - value * guess)
+
+
 def inverse(normal):
     rank = normal.shape[0]
     blocks = [normal[q * SUBS : (q + 1) * SUBS] for q in range(rank // SUBS)]
@@ -179,7 +185,7 @@
         rows, inner = blocks[q], cols[q]
         for k in range(SUBS):
             col = inner[k]
-            pivot = 1.0 / col[k : k + 1]
+            pivot = reciprocal(col[k : k + 1])
             row = jnp.where(lane[0:1] == first + k, 1.0, rows[k : k + 1]) * pivot
             rest = jnp.where(lane == first + k, 0.0, rows) - col * row
             rows = jnp.where(sub == k, row, rest)
@@ -321,14 +327,13 @@
     ra[j] = pbuf[j]
     gram_c = wide_gram(c_all)
 
-    arrived(gb_copies)
-    gram_b = unpacked(functools.reduce(jnp.add, [gb[s] for s in range(n_ja)]), rank)
-    solve_a = inverse(gram_b * gram_c)
-
     arrived(ra_copies)
     ga[j] = functools.reduce(jnp.add, [ra[s] for s in range(n_ja)])
     ga_copies = begin(spread(ga.at[j], ga, j, peers_ja, ga_s, ga_r))
     c_cols = [c_all[:, k : k + 1] for k in range(steps)]
+    arrived(gb_copies)
+    gram_b = unpacked(functools.reduce(jnp.add, [gb[s] for s in range(n_ja)]), rank)
+    solve_a = inverse(gram_b * gram_c)
     arrived(ga_copies)
     summed = stacked(
         [
@@ -361,6 +366,15 @@
     for k in range(steps):
         pieces.append(jnp.concatenate(split(raw_a * c_cols[k]), axis=0).astype(jnp.bfloat16))
     for h in range(cuts_j):
+        if h:
+            arrived(gr_copies)
+            gram_a = unpacked(functools.reduce(jnp.add, [gr[s] for s in range(n_ia)]), rank)
+            lane = lax.broadcasted_iota(jnp.int32, (rank, LANES), 1)
+            sub = lax.broadcasted_iota(jnp.int32, (rank, LANES), 0)
+            squares = jnp.where(lane == sub, gram_a, 0.0)
+            scale_col = 1.0 / jnp.sqrt(jnp.sum(squares, axis=1, keepdims=True) / total_i + EPS)
+            scale_row = 1.0 / jnp.sqrt(jnp.sum(squares, axis=0, keepdims=True) / total_i + EPS)
+            solve_b = inverse(gram_a * scale_col * scale_row * gram_c) * scale_row
         total = jnp.zeros((2 * rank, part_j), jnp.float32)
         for k in range(steps):
             total = total + jnp.dot(
@@ -369,21 +383,8 @@
         total = total[0:rank] + total[rank : 2 * rank]
         for m in range(n_ia // cuts_j):
             pb[h * (n_ia // cuts_j) + m] = total[:, m * piece_j : (m + 1) * piece_j]
-        for step in range(1, n_ia):
-            @pl.when(ring_a[step] // (n_ia // cuts_j) == h)
-            def _():
-                rb_copies[step - 1].start()
-    sends.extend(rb_copies)
+    begin(rb_copies)
     rb[a] = pb[a]
-
-    arrived(gr_copies)
-    gram_a = unpacked(functools.reduce(jnp.add, [gr[s] for s in range(n_ia)]), rank)
-    lane = lax.broadcasted_iota(jnp.int32, (rank, LANES), 1)
-    sub = lax.broadcasted_iota(jnp.int32, (rank, LANES), 0)
-    squares = jnp.where(lane == sub, gram_a, 0.0)
-    scale_col = 1.0 / jnp.sqrt(jnp.sum(squares, axis=1, keepdims=True) / total_i + EPS)
-    scale_row = 1.0 / jnp.sqrt(jnp.sum(squares, axis=0, keepdims=True) / total_i + EPS)
-    solve_b = inverse(gram_a * scale_col * scale_row * gram_c) * scale_row
     new_a = araw[...] * scale_col
     for q in range(groups):
         araw[q * SUBS : (q + 1) * SUBS] = new_a[q * SUBS : (q + 1) * SUBS]

time: 34.3 us -> 37.5 us (1.093)
  Pallas kernels: 33.6 us -> 36.8 us
    pallas_call x1, Pallas kernels: 31.7 us -> 34.9 us  [fused(): pl.pallas_call(functools.partial(kernel, n_ia, n_ja, width_i * n_ia, widt...]
where the time goes in v8:
time: 37.5 us; the launch traced here: 37.4 us
  Pallas kernels  36.8 us (98%)
  between operations  0.64 us (2%)
    pallas_call x1, Pallas kernels, fused(): pl.pallas_call(functools.partial(kernel, n_ia, n_ja, width_i * n_ia, widt...  34.9 us
    pallas_call x1, Pallas kernels, fused(): pl.pallas_call(write_out, out_shape=tuple((jax.ShapeDtypeStruct(r.shape,...  1.87 us

profile of v8, /device:TPU:0, one launch (start us, length us, event | category | flops | bytes accessed | tf_op | source)
XLA Modules:
  0.0 37.4 jit_solution(4408864512741859094)
XLA Ops:
  0.6 34.9 %shard_map.50 = (f32[4,512]{1,0:T(4,128)}, f32[8,512]{1,0:T(8,128)}) custom-call(bf16[8,512,512]{2,1,0:T(8,128)(2,1)} %t_ref.1, f32[8,512]{1,0:T(8,128)} %b_ref.1, f32[1,8]{1,0:T(1,128)} %c_ref.1), custom_call_target="tpu_custom_call" | custom-call | flops 536870912 | bytes 4194304 | tf_op jit(solution)/shard_map/pallas_call | solution.py:483
  35.5 1.9 %shard_map.51 = (f32[4,512]{1,0:T(4,128)}, f32[8,512]{1,0:T(8,128)}) custom-call(f32[4,512]{1,0:T(4,128)} %get-tuple-element.4.a_ref, f32[8,512]{1,0:T(8,128)} %get-tuple-element.5.b_ref), custom_call_target="tpu_custom_call" | custom-call | tf_op jit(solution)/shard_map/pallas_call | solution.py:502

commit v9 on v5

--- a/solution.py
+++ b/solution.py
@@ -164,6 +164,12 @@
     return jnp.concatenate(groups, axis=0)
 
 
+def reciprocal(value):
+    guess = pl.reciprocal(value, approx=True)
+    guess = guess * (2.0 - value * guess)
+    return guess * (2.0 - value * guess)
+
+
 def inverse(normal):
     rank = normal.shape[0]
     blocks = [normal[q * SUBS : (q + 1) * SUBS] for q in range(rank // SUBS)]
@@ -179,7 +185,7 @@
         rows, inner = blocks[q], cols[q]
         for k in range(SUBS):
             col = inner[k]
-            pivot = 1.0 / col[k : k + 1]
+            pivot = reciprocal(col[k : k + 1])
             row = jnp.where(lane[0:1] == first + k, 1.0, rows[k : k + 1]) * pivot
             rest = jnp.where(lane == first + k, 0.0, rows) - col * row
             rows = jnp.where(sub == k, row, rest)
@@ -321,14 +327,13 @@
     ra[j] = pbuf[j]
     gram_c = wide_gram(c_all)
 
-    arrived(gb_copies)
-    gram_b = unpacked(functools.reduce(jnp.add, [gb[s] for s in range(n_ja)]), rank)
-    solve_a = inverse(gram_b * gram_c)
-
     arrived(ra_copies)
     ga[j] = functools.reduce(jnp.add, [ra[s] for s in range(n_ja)])
     ga_copies = begin(spread(ga.at[j], ga, j, peers_ja, ga_s, ga_r))
     c_cols = [c_all[:, k : k + 1] for k in range(steps)]
+    arrived(gb_copies)
+    gram_b = unpacked(functools.reduce(jnp.add, [gb[s] for s in range(n_ja)]), rank)
+    solve_a = inverse(gram_b * gram_c)
     arrived(ga_copies)
     summed = stacked(
         [

time: 34.3 us -> 34.3 us (level)
  no operation moved by 1% of the time
where the time goes in v9:
time: 34.3 us; the launch traced here: 34.2 us
  Pallas kernels  33.6 us (98%)
  between operations  0.64 us (2%)
    pallas_call x1, Pallas kernels, fused(): pl.pallas_call(functools.partial(kernel, n_ia, n_ja, width_i * n_ia, widt...  31.7 us
    pallas_call x1, Pallas kernels, fused(): pl.pallas_call(write_out, out_shape=tuple((jax.ShapeDtypeStruct(r.shape,...  1.87 us

profile of v9, /device:TPU:0, one launch (start us, length us, event | category | flops | bytes accessed | tf_op | source)
XLA Modules:
  0.0 34.2 jit_solution(7963954878436017160)
XLA Ops:
  0.6 31.7 %shard_map.50 = (f32[4,512]{1,0:T(4,128)}, f32[8,512]{1,0:T(8,128)}) custom-call(bf16[8,512,512]{2,1,0:T(8,128)(2,1)} %t_ref.1, f32[8,512]{1,0:T(8,128)} %b_ref.1, f32[1,8]{1,0:T(1,128)} %c_ref.1), custom_call_target="tpu_custom_call" | custom-call | flops 536870912 | bytes 4194304 | tf_op jit(solution)/shard_map/pallas_call | solution.py:487
  32.3 1.9 %shard_map.51 = (f32[4,512]{1,0:T(4,128)}, f32[8,512]{1,0:T(8,128)}) custom-call(f32[4,512]{1,0:T(4,128)} %get-tuple-element.4.a_ref, f32[8,512]{1,0:T(8,128)} %get-tuple-element.5.b_ref), custom_call_target="tpu_custom_call" | custom-call | tf_op jit(solution)/shard_map/pallas_call | solution.py:506
